TPU v7x, 32 devices: a whole 2x2x4 slice. The times are simulated.
32 devices in a mesh: tm: 16 (over z, y, core), region: 2 (over x).
Axes of the slice: x: 2, y: 2, z: 4, core: 2. Of those that a mesh axis runs over, the one named last changes fastest.
Arguments:
- waveform: bfloat16 [192, 131072], P('region', 'tm'), may hold values from -220 to 220
- station_order: int32 [192], P('region'), may hold values from 0 to 191, each once
- library: float32 [128, 24, 200], P('tm'), may hold values from -6 to 6
- owner: int32 [4], replicated, may hold values from 0 to 15
- channels: int32 [4, 8, 24], replicated, may hold values from 0 to 191, as said below
Outputs:
- detection: float32 [4, 8, 131072], P(None, 'region', 'tm')
Inputs may be any that keep to these rules, and one draw needn't show every extreme that they name: `channels`: within one template the 24 station channel ids differ.
All inputs are finite; a program needn't handle non-finite values.
Results may differ from a plain program's by a relative error of at most 0.003.
Values may be sent and summed in bfloat16 or wider, within the bound.
A program may use at most 64 MiB of HBM per device.

v0:
```python
import functools
import jax
import jax.numpy as jnp
from jax import lax
from jax.experimental import pallas as pl
from jax.experimental.pallas import tpu as pltpu
from jax.sharding import PartitionSpec as P

water_level = 4.0
eps = 1e-06
unroll = 4


def scale_kernel(taps, x_ref, inv_ref):
    chans = x_ref.shape[0]
    rows = x_ref.shape[1]
    step = 4
    offsets = lax.broadcasted_iota(jnp.int32, (384, 128), 0) - lax.broadcasted_iota(jnp.int32, (384, 128), 1)
    band = ((offsets >= 0) & (offsets < taps)).astype(jnp.float32).astype(jnp.bfloat16)

    def chunk(i, carry):
        x = x_ref[pl.ds(i * step, step)].reshape(step * rows, 384).astype(jnp.float32)
        square = x * x
        high = square.astype(jnp.bfloat16)
        low = (square - high.astype(jnp.float32)).astype(jnp.bfloat16)
        energy = jnp.dot(high, band, preferred_element_type=jnp.float32)
        energy = energy + jnp.dot(low, band, preferred_element_type=jnp.float32)
        inv_ref[pl.ds(i * step, step)] = lax.rsqrt(energy + taps * water_level).reshape(step, rows, 128)
        return carry

    lax.fori_loop(0, chans // step, chunk, 0)


def pair_kernel(count_ref, code_ref, x_ref, inv_ref, taps_ref, out_ref, acc_ref):
    templates = out_ref.shape[0]
    acc_ref[...] = jnp.zeros_like(acc_ref)
    lane = lax.broadcasted_iota(jnp.int32, (8, 128), 1)
    sub = lax.broadcasted_iota(jnp.int32, (8, 128), 0)

    def one_pair(code):
        template = code & 63
        col = (code >> 6) & 255
        row = code >> 14
        taps = taps_ref[pl.ds(row, 1), :]
        first = jnp.broadcast_to(taps[:, :128], (8, 128))
        second = jnp.broadcast_to(taps[:, 128:], (8, 128))
        first = pltpu.roll(first, 1, 1, stride=1, stride_axis=0)
        second = pltpu.roll(second, 1, 1, stride=1, stride_axis=0)
        zero = jnp.zeros((8, 128), jnp.float32)
        parts = [[], [], []]
        for a in range(16):
            one = pltpu.roll(first, 8 * a, 1) if a else first
            two = pltpu.roll(second, 8 * a, 1) if a else second
            below = lane <= sub + 8 * a
            parts[0].append(jnp.where(below, two, zero))
            parts[1].append(jnp.where(below, one, two))
            parts[2].append(jnp.where(below, zero, one))
        matrix = jnp.concatenate(parts[0] + parts[1] + parts[2], axis=0).astype(jnp.bfloat16)
        product = jnp.dot(x_ref[col], matrix, preferred_element_type=jnp.float32)
        return template, product * inv_ref[col]

    def group(i, carry):
        done = [one_pair(code_ref[i * unroll + u]) for u in range(unroll)]
        for template, value in done:
            acc_ref[template] += value
        return carry

    lax.fori_loop(0, (count_ref[0] + unroll - 1) // unroll, group, 0)
    out_ref[...] = acc_ref[:templates]


def summed_over(value, axis):
    count = lax.axis_size(axis)
    me = lax.axis_index(axis)
    bits = [1 << b for b in range(count.bit_length() - 1)]

    def swap(block, bit):
        return lax.ppermute(block, axis, [(i, i ^ bit) for i in range(count)])

    for bit in bits:
        half = value.shape[0] // 2
        low, high = value[:half], value[half:]
        upper = (me & bit) > 0
        value = jnp.where(upper, high, low) + swap(jnp.where(upper, low, high), bit)
    for bit in reversed(bits):
        upper = (me & bit) > 0
        other = swap(value, bit)
        value = jnp.concatenate([jnp.where(upper, other, value), jnp.where(upper, value, other)], axis=0)
    return value


def finish_kernel(total_time, count, parts_ref, out_ref, sent, got, send_sems, recv_sems):
    me = lax.axis_index("tm")
    region = lax.axis_index("region")
    barrier = pltpu.get_barrier_semaphore()
    for d in range(1, count):
        peer = lax.rem(me + d, count)
        pl.semaphore_signal(barrier, inc=1, device_id=(peer, region), device_id_type=pl.DeviceIdType.MESH)
    held = out_ref.shape[0]
    stacked = parts_ref[0]
    for p in range(1, parts_ref.shape[0]):
        stacked = stacked + parts_ref[p]
    out_ref[...] = stacked
    power = jnp.sum(stacked * stacked, axis=1)
    power = jnp.broadcast_to(jnp.sum(power, axis=1, keepdims=True), (held, 128))
    sent[...] = power
    pl.semaphore_wait(barrier, count - 1)
    copies = []
    for d in range(1, count):
        peer = lax.rem(me + d, count)
        copy = pltpu.make_async_remote_copy(
            src_ref=sent,
            dst_ref=got.at[d - 1],
            send_sem=send_sems.at[d - 1],
            recv_sem=recv_sems.at[d - 1],
            device_id=(peer, region),
            device_id_type=pl.DeviceIdType.MESH,
        )
        copy.start()
        copies.append(copy)
    for copy in copies:
        copy.wait()
    power = power + jnp.sum(got[...], axis=0)
    factor = lax.rsqrt(power / total_time + eps)
    out_ref[...] = out_ref[...] * factor[:, None, :]


def pair_lists(station_order, channels, groups):
    steps, templates, used = channels.shape
    per_group = templates // groups
    length = steps * per_group * used
    grouped = channels.reshape(steps, groups, per_group, used).transpose(1, 0, 2, 3).reshape(groups, length)
    slot = jnp.arange(length, dtype=jnp.int32)
    step = slot // (per_group * used)
    inner = slot % (per_group * used)
    match = (grouped[:, :, None] == station_order[None, None, :]).astype(jnp.int32)
    local = jnp.sum(match, axis=2)
    col = jnp.sum(match * jnp.arange(station_order.shape[0], dtype=jnp.int32), axis=2)
    before = (slot[:, None] > slot[None, :]).astype(jnp.int32)
    place = jnp.sum(before[None] * local[:, None, :], axis=2)
    count = jnp.sum(local, axis=1)
    row = step * (templates * used) + jnp.arange(groups, dtype=jnp.int32)[:, None] * (per_group * used) + inner
    template = slot // used
    code = (row << 14) | (col << 6) | template
    chosen = ((place[:, None, :] == slot[None, :, None]) & (local[:, None, :] > 0)).astype(jnp.int32)
    packed = jnp.sum(chosen * code[:, None, :], axis=2)
    packed = jnp.where(slot[None, :] < count[:, None], packed, steps * per_group)
    return packed, count


def body(waveform, station_order, library, owner, channels):
    chan_local, time_local = waveform.shape
    num_blocks = time_local // 128
    steps, templates, used = channels.shape
    tap_count = library.shape[2]
    tm_size = lax.axis_size("tm")
    regions = lax.axis_size("region")
    per_group = templates // regions
    held = steps * per_group
    total_time = time_local * tm_size

    rim = lax.ppermute(waveform[:, :256], "tm", [(i, i - 1) for i in range(1, tm_size)])
    rim = jnp.where(jnp.arange(256)[None, :] < tap_count - 1, rim, jnp.zeros_like(rim))

    centred = library - jnp.mean(library, axis=2, keepdims=True)
    normed = centred / jnp.sqrt(jnp.sum(centred * centred, axis=2, keepdims=True) + eps)
    normed = jnp.pad(normed.astype(jnp.bfloat16).reshape(templates * used, tap_count), ((0, 0), (0, 256 - tap_count)))
    mine = (owner == lax.axis_index("tm"))[:, None, None]
    taps = jnp.where(mine, normed[None], jnp.zeros_like(normed)[None])
    taps = summed_over(taps.reshape(steps * templates * used, 256), "tm")
    taps = jnp.flip(taps, axis=1).astype(jnp.float32)

    blocked = waveform.reshape(chan_local, num_blocks, 128)
    rim_blocks = rim.reshape(chan_local, 2, 128)
    extended = jnp.concatenate([blocked, rim_blocks], axis=1)
    windows = jnp.concatenate([extended[:, i : i + num_blocks] for i in range(3)], axis=2)

    vmem = pl.BlockSpec(memory_space=pltpu.VMEM)
    smem = pl.BlockSpec(memory_space=pltpu.SMEM)
    inv_scale = pl.pallas_call(
        functools.partial(scale_kernel, tap_count),
        out_shape=jax.ShapeDtypeStruct((chan_local, num_blocks, 128), jnp.float32),
        in_specs=[vmem],
        out_specs=vmem,
        compiler_params=pltpu.CompilerParams(vmem_limit_bytes=40 * 2**20),
        name="scales",
    )(windows)

    codes, counts = pair_lists(station_order, channels, regions)
    me = lax.axis_index("region")

    def partial_sums(group):
        return pl.pallas_call(
            pair_kernel,
            out_shape=jax.ShapeDtypeStruct((held, num_blocks, 128), jnp.float32),
            in_specs=[smem, smem, vmem, vmem, vmem],
            out_specs=vmem,
            scratch_shapes=[pltpu.VMEM((held + 1, num_blocks, 128), jnp.float32)],
            compiler_params=pltpu.CompilerParams(vmem_limit_bytes=40 * 2**20),
            cost_estimate=pl.CostEstimate(flops=held * used * 64 * 384 * 256, bytes_accessed=9 * 2**20, transcendentals=0),
            name="pairs",
        )(lax.dynamic_slice_in_dim(counts, group, 1), lax.dynamic_index_in_dim(codes, group, 0, False), windows, inv_scale, taps)

    arrived = []
    for shift in range(1, regions):
        part = partial_sums((me + shift) % regions)
        arrived.append(lax.ppermute(part, "region", [(i, (i + shift) % regions) for i in range(regions)]))
    arrived.append(partial_sums(me))
    result = pl.pallas_call(
        functools.partial(finish_kernel, total_time, tm_size),
        out_shape=jax.ShapeDtypeStruct((held, num_blocks, 128), jnp.float32),
        in_specs=[vmem],
        out_specs=vmem,
        scratch_shapes=[
            pltpu.VMEM((held, 128), jnp.float32),
            pltpu.VMEM((tm_size - 1, held, 128), jnp.float32),
            pltpu.SemaphoreType.DMA((tm_size - 1,)),
            pltpu.SemaphoreType.DMA((tm_size - 1,)),
        ],
        compiler_params=pltpu.CompilerParams(
            collective_id=0, has_side_effects=True, vmem_limit_bytes=40 * 2**20
        ),
        name="finish",
    )(jnp.stack(arrived))
    return result.reshape(steps, per_group, time_local)


def solution(mesh):
    in_specs = (P("region", "tm"), P("region"), P("tm", None, None), P(), P())
    out_specs = P(None, "region", "tm")
    return jax.shard_map(body, mesh=mesh, in_specs=in_specs, out_specs=out_specs, check_vma=False)
```

profile of v0, /device:TPU:0, one launch (start us, length us, event | category | flops | bytes accessed | tf_op | source)
XLA Modules:
  0.0 104.2 jit_solution(12366189651903683983)
XLA Ops:
  0.0 0.0 copy-start.3
  0.0 0.0 copy-start.4
  0.0 1.4 %slice.35 = bf16[96,256]{1,0:T(8,128)(2,1)} slice(bf16[96,8192]{1,0:T(8,128)(2,1)} %param.5), slice={[0:96], [0:256]} | slice | bytes 98304 | tf_op jit(solution)/shard_map/slice | solution.py:162
  1.5 1.3 %collective-permute-start = (bf16[96,256]{1,0:T(8,128)(2,1)}, bf16[96,256]{1,0:T(8,128)(2,1)}, u32[]{:S(2)}, u32[]{:S(2)}) collective-permute-start(bf16[96,256]{1,0:T(8,128)(2,1)} %slice.35), channel_id=1, source_target_pairs={{2,0},{4,2},{6,4},{8,6},{10,8},{12,10},{14,12},{16,14},{18,16},{20... | collective-permute-start | bytes 147464 | tf_op jit(solution)/shard_map/ppermute | solution.py:162
  2.7 0.7 broadcast_compare_fusion.1
  3.4 1.0 reduce_sum.68
  4.4 1.1 %multiply_reduce_fusion.1 = f32[8,24]{1,0:T(8,128)S(1)} fusion(f32[8,24,200]{2,1,0:T(8,128)} %param.7, f32[8,24]{1,0:T(8,128)S(1)} %broadcast_multiply_fusion), kind=kLoop, calls=%fused_computation.17 | loop fusion | flops 115008 | bytes 155136 | tf_op jit(solution)/shard_map/reduce_sum | solution.py:166
  5.6 1.0 %divide_convert_fusion = bf16[8,24,200]{2,1,0:T(8,128)(2,1)S(1)} fusion(f32[8,24,200]{2,1,0:T(8,128)} %param.7, f32[8,24]{1,0:T(8,128)S(1)} %add_sqrt_fusion, f32[8,24]{1,0:T(8,128)S(1)} %broadcast_multiply_fusion), kind=kLoop, calls=%fused_computation.16 | loop fusion | flops 115200 | bytes 231936 | tf_op jit(solution)/shard_map/convert_element_type | solution.py:167
  6.7 0.0 copy-start.2
  6.7 0.1 broadcast_select_fusion
  6.8 1.2 %collective-permute-start.1 = (bf16[384,256]{1,0:T(8,128)(2,1)S(1)}, bf16[384,256]{1,0:T(8,128)(2,1)S(1)}, u32[]{:S(2)}, u32[]{:S(2)}) collective-permute-start(bf16[384,256]{1,0:T(8,128)(2,1)S(1)} %bitcast.18), channel_id=1, source_target_pairs={{0,2},{2,0},{4,6},{6,4},{8,10},{10,8},{12,14},{14,12},{16,18},{18,... | collective-permute-start | bytes 589832 | tf_op jit(solution)/shard_map/ppermute | solution.py:78
  8.1 0.0 copy-done.3
  8.1 0.1 eq.38
  8.2 0.0 copy-done.4
  8.2 0.3 convert_reduce_fusion
  8.5 0.1 or_or_fusion
  8.6 0.2 multiply_reduce_fusion
  8.8 0.3 select_reduce_fusion
  9.1 0.0 collective-permute-done.1
  9.2 3.0 %collective-permute-start.2 = (bf16[192,256]{1,0:T(8,128)(2,1)S(1)}, bf16[192,256]{1,0:T(8,128)(2,1)S(1)}, u32[]{:S(2)}, u32[]{:S(2)}) collective-permute-start(bf16[192,256]{1,0:T(8,128)(2,1)S(1)} %broadcast_select_fusion.7), channel_id=1, source_target_pairs={{0,4},{2,6},{4,0},{6,2},{8,12},{10,14},{12,8},{14,10},{16,20},{18,... | collective-permute-start | bytes 294920 | tf_op jit(solution)/shard_map/ppermute | solution.py:78
  12.2 0.1 compare_select_fusion.1
  12.3 0.0 copy-done.2
  12.3 0.4 copy.8
  12.7 2.8 %collective-permute-done.2 = bf16[192,256]{1,0:T(8,128)(2,1)S(1)} collective-permute-done((bf16[192,256]{1,0:T(8,128)(2,1)S(1)}, bf16[192,256]{1,0:T(8,128)(2,1)S(1)}, u32[]{:S(2)}, u32[]{:S(2)}) %collective-permute-start.2) | collective-permute-done | bytes 98336 | tf_op jit(solution)/shard_map/ppermute | solution.py:78
  15.5 2.4 %collective-permute-start.3 = (bf16[96,256]{1,0:T(8,128)(2,1)S(1)}, bf16[96,256]{1,0:T(8,128)(2,1)S(1)}, u32[]{:S(2)}, u32[]{:S(2)}) collective-permute-start(bf16[96,256]{1,0:T(8,128)(2,1)S(1)} %broadcast_select_fusion.10), channel_id=1, source_target_pairs={{0,8},{2,10},{4,12},{6,14},{8,0},{10,2},{12,4},{14,6},{16,24},{18,... | collective-permute-start | bytes 147464 | tf_op jit(solution)/shard_map/ppermute | solution.py:78
  17.9 1.4 %constant_dynamic-update-slice_fusion.1 = bf16[96,66,128]{2,1,0:T(8,128)(2,1)} fusion(bf16[96,64,128]{2,1,0:T(8,128)(2,1)S(1)} %bitcast.13), kind=kLoop, calls=%fused_computation.39 | loop fusion | bytes 3145728
  19.3 0.6 collective-permute-done.3
  20.0 3.1 %collective-permute-start.4 = (bf16[48,256]{1,0:T(8,128)(2,1)S(1)}, bf16[48,256]{1,0:T(8,128)(2,1)S(1)}, u32[]{:S(2)}, u32[]{:S(2)}) collective-permute-start(bf16[48,256]{1,0:T(8,128)(2,1)S(1)} %broadcast_select_fusion.14), channel_id=1, source_target_pairs={{0,16},{2,18},{4,20},{6,22},{8,24},{10,26},{12,28},{14,30},{16,0},... | collective-permute-start | bytes 73736 | tf_op jit(solution)/shard_map/ppermute | solution.py:78
  23.1 0.7 fusion.13
  23.8 1.1 %collective-permute-done.4 = bf16[48,256]{1,0:T(8,128)(2,1)S(1)} collective-permute-done((bf16[48,256]{1,0:T(8,128)(2,1)S(1)}, bf16[48,256]{1,0:T(8,128)(2,1)S(1)}, u32[]{:S(2)}, u32[]{:S(2)}) %collective-permute-start.4) | collective-permute-done | bytes 24608 | tf_op jit(solution)/shard_map/ppermute | solution.py:78
  24.9 3.0 %collective-permute-start.5 = (bf16[48,256]{1,0:T(8,128)(2,1)S(1)}, bf16[48,256]{1,0:T(8,128)(2,1)S(1)}, u32[]{:S(2)}, u32[]{:S(2)}) collective-permute-start(bf16[48,256]{1,0:T(8,128)(2,1)S(1)} %select_add_fusion.2), channel_id=1, source_target_pairs={{0,16},{2,18},{4,20},{6,22},{8,24},{10,26},{12,28},{14,30},{16,0},... | collective-permute-start | bytes 73736 | tf_op jit(solution)/shard_map/ppermute | solution.py:78
  27.9 0.0 collective-permute-done
  27.9 0.8 broadcast_select_fusion.11
  28.7 1.0 collective-permute-done.5
  29.7 2.3 %collective-permute-start.6 = (bf16[96,256]{1,0:T(8,128)(2,1)S(1)}, bf16[96,256]{1,0:T(8,128)(2,1)S(1)}, u32[]{:S(2)}, u32[]{:S(2)}) collective-permute-start(bf16[96,256]{1,0:T(8,128)(2,1)S(1)} %pad_maximum_fusion.5), channel_id=1, source_target_pairs={{0,8},{2,10},{4,12},{6,14},{8,0},{10,2},{12,4},{14,6},{16,24},{18,... | collective-permute-start | bytes 147464 | tf_op jit(solution)/shard_map/ppermute | solution.py:78
  32.0 0.7 constant_dynamic-update-slice_fusion
  32.7 1.4 %collective-permute-done.6 = bf16[96,256]{1,0:T(8,128)(2,1)S(1)} collective-permute-done((bf16[96,256]{1,0:T(8,128)(2,1)S(1)}, bf16[96,256]{1,0:T(8,128)(2,1)S(1)}, u32[]{:S(2)}, u32[]{:S(2)}) %collective-permute-start.6) | collective-permute-done | bytes 49184 | tf_op jit(solution)/shard_map/ppermute | solution.py:78
  34.2 1.2 %collective-permute-start.7 = (bf16[192,256]{1,0:T(8,128)(2,1)S(1)}, bf16[192,256]{1,0:T(8,128)(2,1)S(1)}, u32[]{:S(2)}, u32[]{:S(2)}) collective-permute-start(bf16[192,256]{1,0:T(8,128)(2,1)S(1)} %pad_maximum_fusion.4), channel_id=1, source_target_pairs={{0,4},{2,6},{4,0},{6,2},{8,12},{10,14},{12,8},{14,10},{16,20},{18,... | collective-permute-start | bytes 294920 | tf_op jit(solution)/shard_map/ppermute | solution.py:78
  35.4 3.8 %fusion.12 = (bf16[96,64,128]{2,1,0:T(8,128)(2,1)S(1)}, bf16[96,64,128]{2,1,0:T(8,128)(2,1)S(1)}) fusion(bf16[96,66,128]{2,1,0:T(8,128)(2,1)} %constant_dynamic-update-slice_fusion), kind=kLoop, calls=%fused_computation.66 | loop fusion | bytes 6291456 | tf_op jit(solution)/shard_map/slice | solution.py:176
  39.2 0.0 collective-permute-done.7
  39.3 0.1 collective-permute-start.8
  39.4 0.7 pad_maximum_fusion.x_ref
  40.1 0.0 copy-start
  40.1 6.3 %scales.1.inv_ref = f32[96,64,128]{2,1,0:T(8,128)S(1)} custom-call(bf16[96,64,384]{2,1,0:T(8,128)(2,1)S(1)} %pad_maximum_fusion.x_ref), custom_call_target="tpu_custom_call" | custom-call | tf_op jit(solution)/shard_map/scales/pallas_call | solution.py:180
  46.4 0.0 copy-done
  46.4 0.0 collective-permute-done.8
  46.4 0.1 broadcast_select_fusion.4
  46.5 4.3 %rev.4 = bf16[768,256]{1,0:T(8,128)(2,1)} reverse(bf16[768,256]{1,0:T(8,128)(2,1)S(1)} %pad_maximum_fusion.2), dimensions={1} | reverse | bytes 786432 | tf_op jit(solution)/shard_map/jit(_flip)/rev | solution.py:171
  50.9 1.0 %convert_element_type.22.taps_ref = f32[768,256]{1,0:T(8,128)S(1)} convert(bf16[768,256]{1,0:T(8,128)(2,1)} %rev.4) | non-fusion elementwise | flops 196608 | bytes 1179648 | tf_op jit(solution)/shard_map/convert_element_type | solution.py:171
  51.9 0.0 copy-start.1
  51.9 2.3 %copy-done.1 = bf16[96,64,384]{2,1,0:T(8,128)(2,1)S(1)} copy-done((bf16[96,64,384]{2,1,0:T(8,128)(2,1)S(1)}, bf16[96,64,384]{2,1,0:T(8,128)(2,1)}, u32[]{:S(2)}) %copy-start.1) | copy-done | bytes 4718616
  54.2 17.8 %pairs.2 = f32[16,64,128]{2,1,0:T(8,128)S(1)} custom-call(s32[1]{0:T(128)} %get-tuple-element.22.count_ref, s32[384]{0:T(512)S(1)} %get-tuple-element.8.code_ref, bf16[96,64,384]{2,1,0:T(8,128)(2,1)S(1)} %copy-done.1, f32[96,64,128]{2,1,0:T(8,128)S(1)} %scales.1.inv_ref, f32[768,256]{1,0:T(8,128)S(1)} %convert_element_type.22.taps_ref), custom_call_target="tpu_custom_call" | custom-call | flops 2415919104 | bytes 9437184 | tf_op jit(solution)/shard_map/pairs/pallas_call | solution.py:193
  72.1 2.3 %collective-permute-start.9 = (f32[16,64,128]{2,1,0:T(8,128)S(1)}, f32[16,64,128]{2,1,0:T(8,128)S(1)}, u32[]{:S(2)}, u32[]{:S(2)}) collective-permute-start(f32[16,64,128]{2,1,0:T(8,128)S(1)} %pairs.2), channel_id=1, source_target_pairs={{0,1},{1,0},{2,3},{3,2},{4,5},{5,4},{6,7},{7,6},{8,9},{9,8},{10,11... | collective-permute-start | bytes 1572872 | tf_op jit(solution)/shard_map/ppermute | solution.py:207
  74.4 20.2 %pairs.3 = f32[16,64,128]{2,1,0:T(8,128)S(1)} custom-call(s32[1]{0:T(128)} %get-tuple-element.23.count_ref, s32[384]{0:T(512)S(1)} %get-tuple-element.9.code_ref, bf16[96,64,384]{2,1,0:T(8,128)(2,1)S(1)} %copy-done.1, f32[96,64,128]{2,1,0:T(8,128)S(1)} %scales.1.inv_ref, f32[768,256]{1,0:T(8,128)S(1)} %convert_element_type.22.taps_ref), custom_call_target="tpu_custom_call" | custom-call | flops 2415919104 | bytes 9437184 | tf_op jit(solution)/shard_map/pairs/pallas_call | solution.py:193
  94.6 0.0 collective-permute-done.9
  94.6 0.1 pad_maximum_fusion.1.parts_ref
  94.7 8.4 %finish.1 = f32[16,64,128]{2,1,0:T(8,128)S(1)} custom-call(f32[2,16,64,128]{3,2,1,0:T(8,128)S(1)} %pad_maximum_fusion.1.parts_ref), custom_call_target="tpu_custom_call" | custom-call | tf_op jit(solution)/shard_map/finish/pallas_call | solution.py:209
  103.2 1.0 reshape.153
  (27 shorter events, 0.4 us)
Async XLA Ops:
  0.0 8.1 %copy-start.3 = (s32[4,8,24]{2,1,0:T(8,128)S(1)}, s32[4,8,24]{2,1,0:T(8,128)}, u32[]{:S(2)}) copy-start(s32[4,8,24]{2,1,0:T(8,128)} %param.9) | copy-start | bytes 9220
  0.0 8.2 %copy-start.4 = (s32[96]{0:T(128)S(1)}, s32[96]{0:T(128)}, u32[]{:S(2)}) copy-start(s32[96]{0:T(128)} %param.6) | copy-start | bytes 1156
  1.5 26.5 %collective-permute-start = (bf16[96,256]{1,0:T(8,128)(2,1)}, bf16[96,256]{1,0:T(8,128)(2,1)}, u32[]{:S(2)}, u32[]{:S(2)}) collective-permute-start(bf16[96,256]{1,0:T(8,128)(2,1)} %slice.35), channel_id=1, source_target_pairs={{2,0},{4,2},{6,4},{8,6},{10,8},{12,10},{14,12},{16,14},{18,16},{20... | collective-permute-start | bytes 147464 | tf_op jit(solution)/shard_map/ppermute | solution.py:162
  6.7 5.6 %copy-start.2 = (bf16[96,8192]{1,0:T(8,128)(2,1)S(1)}, bf16[96,8192]{1,0:T(8,128)(2,1)}, u32[]{:S(2)}) copy-start(bf16[96,8192]{1,0:T(8,128)(2,1)} %param.5) | copy-start | bytes 4718596
  6.8 2.3 %collective-permute-start.1 = (bf16[384,256]{1,0:T(8,128)(2,1)S(1)}, bf16[384,256]{1,0:T(8,128)(2,1)S(1)}, u32[]{:S(2)}, u32[]{:S(2)}) collective-permute-start(bf16[384,256]{1,0:T(8,128)(2,1)S(1)} %bitcast.18), channel_id=1, source_target_pairs={{0,2},{2,0},{4,6},{6,4},{8,10},{10,8},{12,14},{14,12},{16,18},{18,... | collective-permute-start | bytes 589832 | tf_op jit(solution)/shard_map/ppermute | solution.py:78
  9.2 6.3 %collective-permute-start.2 = (bf16[192,256]{1,0:T(8,128)(2,1)S(1)}, bf16[192,256]{1,0:T(8,128)(2,1)S(1)}, u32[]{:S(2)}, u32[]{:S(2)}) collective-permute-start(bf16[192,256]{1,0:T(8,128)(2,1)S(1)} %broadcast_select_fusion.7), channel_id=1, source_target_pairs={{0,4},{2,6},{4,0},{6,2},{8,12},{10,14},{12,8},{14,10},{16,20},{18,... | collective-permute-start | bytes 294920 | tf_op jit(solution)/shard_map/ppermute | solution.py:78
  15.5 4.4 %collective-permute-start.3 = (bf16[96,256]{1,0:T(8,128)(2,1)S(1)}, bf16[96,256]{1,0:T(8,128)(2,1)S(1)}, u32[]{:S(2)}, u32[]{:S(2)}) collective-permute-start(bf16[96,256]{1,0:T(8,128)(2,1)S(1)} %broadcast_select_fusion.10), channel_id=1, source_target_pairs={{0,8},{2,10},{4,12},{6,14},{8,0},{10,2},{12,4},{14,6},{16,24},{18,... | collective-permute-start | bytes 147464 | tf_op jit(solution)/shard_map/ppermute | solution.py:78
  20.0 4.9 %collective-permute-start.4 = (bf16[48,256]{1,0:T(8,128)(2,1)S(1)}, bf16[48,256]{1,0:T(8,128)(2,1)S(1)}, u32[]{:S(2)}, u32[]{:S(2)}) collective-permute-start(bf16[48,256]{1,0:T(8,128)(2,1)S(1)} %broadcast_select_fusion.14), channel_id=1, source_target_pairs={{0,16},{2,18},{4,20},{6,22},{8,24},{10,26},{12,28},{14,30},{16,0},... | collective-permute-start | bytes 73736 | tf_op jit(solution)/shard_map/ppermute | solution.py:78
  24.9 4.8 %collective-permute-start.5 = (bf16[48,256]{1,0:T(8,128)(2,1)S(1)}, bf16[48,256]{1,0:T(8,128)(2,1)S(1)}, u32[]{:S(2)}, u32[]{:S(2)}) collective-permute-start(bf16[48,256]{1,0:T(8,128)(2,1)S(1)} %select_add_fusion.2), channel_id=1, source_target_pairs={{0,16},{2,18},{4,20},{6,22},{8,24},{10,26},{12,28},{14,30},{16,0},... | collective-permute-start | bytes 73736 | tf_op jit(solution)/shard_map/ppermute | solution.py:78
  29.7 4.4 %collective-permute-start.6 = (bf16[96,256]{1,0:T(8,128)(2,1)S(1)}, bf16[96,256]{1,0:T(8,128)(2,1)S(1)}, u32[]{:S(2)}, u32[]{:S(2)}) collective-permute-start(bf16[96,256]{1,0:T(8,128)(2,1)S(1)} %pad_maximum_fusion.5), channel_id=1, source_target_pairs={{0,8},{2,10},{4,12},{6,14},{8,0},{10,2},{12,4},{14,6},{16,24},{18,... | collective-permute-start | bytes 147464 | tf_op jit(solution)/shard_map/ppermute | solution.py:78
  34.2 5.0 %collective-permute-start.7 = (bf16[192,256]{1,0:T(8,128)(2,1)S(1)}, bf16[192,256]{1,0:T(8,128)(2,1)S(1)}, u32[]{:S(2)}, u32[]{:S(2)}) collective-permute-start(bf16[192,256]{1,0:T(8,128)(2,1)S(1)} %pad_maximum_fusion.4), channel_id=1, source_target_pairs={{0,4},{2,6},{4,0},{6,2},{8,12},{10,14},{12,8},{14,10},{16,20},{18,... | collective-permute-start | bytes 294920 | tf_op jit(solution)/shard_map/ppermute | solution.py:78
  39.3 7.1 %collective-permute-start.8 = (bf16[384,256]{1,0:T(8,128)(2,1)S(1)}, bf16[384,256]{1,0:T(8,128)(2,1)S(1)}, u32[]{:S(2)}, u32[]{:S(2)}) collective-permute-start(bf16[384,256]{1,0:T(8,128)(2,1)S(1)} %pad_maximum_fusion.3), channel_id=1, source_target_pairs={{0,2},{2,0},{4,6},{6,4},{8,10},{10,8},{12,14},{14,12},{16,18},{18,... | collective-permute-start | bytes 589832 | tf_op jit(solution)/shard_map/ppermute | solution.py:78
  40.1 6.3 %copy-start = (bf16[96,64,384]{2,1,0:T(8,128)(2,1)}, bf16[96,64,384]{2,1,0:T(8,128)(2,1)S(1)}, u32[]{:S(2)}) copy-start(bf16[96,64,384]{2,1,0:T(8,128)(2,1)S(1)} %pad_maximum_fusion.x_ref) | copy-start | bytes 14155780
  51.9 2.3 %copy-start.1 = (bf16[96,64,384]{2,1,0:T(8,128)(2,1)S(1)}, bf16[96,64,384]{2,1,0:T(8,128)(2,1)}, u32[]{:S(2)}) copy-start(bf16[96,64,384]{2,1,0:T(8,128)(2,1)} %copy-done) | copy-start | bytes 14155780
  72.1 22.5 %collective-permute-start.9 = (f32[16,64,128]{2,1,0:T(8,128)S(1)}, f32[16,64,128]{2,1,0:T(8,128)S(1)}, u32[]{:S(2)}, u32[]{:S(2)}) collective-permute-start(f32[16,64,128]{2,1,0:T(8,128)S(1)} %pairs.2), channel_id=1, source_target_pairs={{0,1},{1,0},{2,3},{3,2},{4,5},{5,4},{6,7},{7,6},{8,9},{9,8},{10,11... | collective-permute-start | bytes 1572872 | tf_op jit(solution)/shard_map/ppermute | solution.py:207
where the time goes:
time: 105 us; the launch traced here: 104 us
  Pallas kernels  52.7 us (50%)
  starting transfers between devices  19.9 us (19%)
  local copies, waits for them, and re-layouts  16.3 us (16%)
  other arithmetic  7.98 us (8%)
  waiting for transfers between devices  6.93 us (7%)
    pallas_call x2, Pallas kernels, partial_sums(): pl.pallas_call(pair_kernel, out_shape=jax.ShapeDtypeStruct((held, num_blo...  38.1 us
    ppermute x8, starting transfers between devices, swap(): return lax.ppermute(block, axis, [(i, i ^ bit) for i in range(count)])  16.3 us
    pallas_call x1, Pallas kernels, body(): pl.pallas_call(functools.partial(finish_kernel, total_time, tm_size), out...  8.4 us
    ppermute x8, waiting for transfers between devices, swap(): return lax.ppermute(block, axis, [(i, i ^ bit) for i in range(count)])  6.92 us
    pallas_call x1, Pallas kernels, body(): pl.pallas_call(functools.partial(scale_kernel, tap_count), out_shape=jax....  6.28 us
    rev x1, local copies, waits for them, and re-layouts, body(): taps = jnp.flip(taps, axis=1).astype(jnp.float32)  4.31 us
    unnamed x12, local copies, waits for them, and re-layouts  4.21 us
    slice x1, local copies, waits for them, and re-layouts, body(): extended[:, i:i + num_blocks]  3.81 us
  transfers between devices with their start and end apart: 10, of which 5 were waited for; matrix products, arithmetic and copies ran while one was open for 13% of the time, Pallas kernels for 25%

commit v1 on v0

v1 whole, which is shorter than its diff:
```python
import functools
import jax
import jax.numpy as jnp
from jax import lax
from jax.experimental import pallas as pl
from jax.experimental.pallas import tpu as pltpu
from jax.sharding import PartitionSpec as P

water_level = 4.0
eps = 1e-06
unroll = 8


def prepare_kernel(steps, count, owner_ref, library_ref, x_ref, inv_ref, out_ref, part, full, got, send_sems, recv_sems):
    me = lax.axis_index("tm")
    region = lax.axis_index("region")
    barrier = pltpu.get_barrier_semaphore()
    for d in range(1, count):
        peer = lax.rem(me + d, count)
        pl.semaphore_signal(barrier, inc=1, device_id=(peer, region), device_id_type=pl.DeviceIdType.MESH)

    panel = library_ref[...]
    taps = panel.shape[1]
    rows = panel.shape[0] // 16
    centred = panel - jnp.sum(panel, axis=1, keepdims=True) / taps
    normed = centred / jnp.sqrt(jnp.sum(centred * centred, axis=1, keepdims=True) + eps)
    mirror = lax.broadcasted_iota(jnp.int32, (taps, 256), 0) + lax.broadcasted_iota(jnp.int32, (taps, 256), 1)
    mirror = (mirror == 255).astype(jnp.float32).astype(jnp.bfloat16)
    turned = jnp.dot(normed.astype(jnp.bfloat16), mirror, preferred_element_type=jnp.float32)
    turned = turned.reshape(rows, 16, 256)
    if part.shape[0] > steps * rows:
        part[steps * rows :] = jnp.zeros((part.shape[0] - steps * rows, 16, 256), jnp.bfloat16)
    for s in range(steps):
        mine = jnp.where(owner_ref[s] == me, jnp.float32(1), jnp.float32(0))
        part[s * rows : (s + 1) * rows] = (turned * mine).astype(jnp.bfloat16)

    chans = x_ref.shape[0]
    blocks = x_ref.shape[1]
    group = 4
    chunks = chans // group
    offsets = lax.broadcasted_iota(jnp.int32, (384, 128), 0) - lax.broadcasted_iota(jnp.int32, (384, 128), 1)
    band = ((offsets >= 0) & (offsets < taps)).astype(jnp.float32).astype(jnp.bfloat16)

    def chunk(i, carry):
        x = x_ref[pl.ds(i * group, group)].reshape(group * blocks, 384).astype(jnp.float32)
        square = x * x
        high = square.astype(jnp.bfloat16)
        low = (square - high.astype(jnp.float32)).astype(jnp.bfloat16)
        energy = jnp.dot(high, band, preferred_element_type=jnp.float32)
        energy = energy + jnp.dot(low, band, preferred_element_type=jnp.float32)
        inv_ref[pl.ds(i * group, group)] = lax.rsqrt(energy + taps * water_level).reshape(group, blocks, 128)
        return carry

    phases = 2

    def scales(phase):
        lax.fori_loop(phase * chunks // phases, (phase + 1) * chunks // phases, chunk, 0)

    pl.semaphore_wait(barrier, count - 1)
    size = part.shape[0] // count
    own = pl.ds(me * size, size)

    def exchange(phase, source, target):
        copies = []
        for d in range(1, count):
            peer = lax.rem(me + d, count)
            copy = pltpu.make_async_remote_copy(
                src_ref=source(peer),
                dst_ref=target(d),
                send_sem=send_sems.at[phase, d - 1],
                recv_sem=recv_sems.at[phase, d - 1],
                device_id=(peer, region),
                device_id_type=pl.DeviceIdType.MESH,
            )
            copy.start()
            copies.append(copy)
        scales(phase)
        for copy in copies:
            copy.wait()

    exchange(0, lambda peer: part.at[pl.ds(peer * size, size)], lambda d: got.at[d - 1])
    total = part[own].astype(jnp.float32)
    for d in range(1, count):
        total = total + got[d - 1].astype(jnp.float32)
    full[own] = total.astype(jnp.bfloat16)
    exchange(1, lambda peer: full.at[own], lambda d: full.at[own])
    out_ref[...] = full[...].astype(jnp.float32)


def pair_kernel(code_ref, x_ref, inv_ref, taps_ref, out_ref, acc_ref, list_ref):
    templates = out_ref.shape[0]

    def compact(i, filled):
        code = code_ref[i]
        list_ref[filled] = code
        return filled + jnp.where(code >= 0, 1, 0)

    count = lax.fori_loop(0, code_ref.shape[0], compact, 0, unroll=8)
    for u in range(unroll):
        list_ref[count + u] = templates
    acc_ref[...] = jnp.zeros_like(acc_ref)
    lane = lax.broadcasted_iota(jnp.int32, (8, 128), 1)
    sub = lax.broadcasted_iota(jnp.int32, (8, 128), 0)

    def one_pair(code):
        template = code & 63
        col = (code >> 6) & 255
        row = code >> 14
        taps = taps_ref[pl.ds(row, 1), :]
        first = jnp.broadcast_to(taps[:, :128], (8, 128))
        second = jnp.broadcast_to(taps[:, 128:], (8, 128))
        first = pltpu.roll(first, 1, 1, stride=1, stride_axis=0)
        second = pltpu.roll(second, 1, 1, stride=1, stride_axis=0)
        zero = jnp.zeros((8, 128), jnp.float32)
        parts = [[], [], []]
        for a in range(16):
            one = pltpu.roll(first, 8 * a, 1) if a else first
            two = pltpu.roll(second, 8 * a, 1) if a else second
            below = lane <= sub + 8 * a
            parts[0].append(jnp.where(below, two, zero))
            parts[1].append(jnp.where(below, one, two))
            parts[2].append(jnp.where(below, zero, one))
        matrix = jnp.concatenate(parts[0] + parts[1] + parts[2], axis=0).astype(jnp.bfloat16)
        product = jnp.dot(x_ref[col], matrix, preferred_element_type=jnp.float32)
        return template, product * inv_ref[col]

    def group(i, carry):
        done = [one_pair(list_ref[i * unroll + u]) for u in range(unroll)]
        for template, value in done:
            acc_ref[template] += value
        return carry

    lax.fori_loop(0, (count + unroll - 1) // unroll, group, 0)
    out_ref[...] = acc_ref[:templates]


def finish_kernel(total_time, count, *refs):
    *parts, out_ref, sent, got, send_sems, recv_sems = refs
    me = lax.axis_index("tm")
    region = lax.axis_index("region")
    barrier = pltpu.get_barrier_semaphore()
    for d in range(1, count):
        peer = lax.rem(me + d, count)
        pl.semaphore_signal(barrier, inc=1, device_id=(peer, region), device_id_type=pl.DeviceIdType.MESH)
    held = out_ref.shape[0]
    stacked = parts[0][...]
    for other in parts[1:]:
        stacked = stacked + other[...]
    out_ref[...] = stacked
    power = jnp.sum(stacked * stacked, axis=1)
    power = jnp.broadcast_to(jnp.sum(power, axis=1, keepdims=True), (held, 128))
    sent[...] = power
    pl.semaphore_wait(barrier, count - 1)
    copies = []
    for d in range(1, count):
        peer = lax.rem(me + d, count)
        copy = pltpu.make_async_remote_copy(
            src_ref=sent,
            dst_ref=got.at[d - 1],
            send_sem=send_sems.at[d - 1],
            recv_sem=recv_sems.at[d - 1],
            device_id=(peer, region),
            device_id_type=pl.DeviceIdType.MESH,
        )
        copy.start()
        copies.append(copy)
    for copy in copies:
        copy.wait()
    power = power + jnp.sum(got[...], axis=0)
    factor = lax.rsqrt(power / total_time + eps)
    out_ref[...] = out_ref[...] * factor[:, None, :]


def pair_lists(station_order, channels, groups):
    steps, templates, used = channels.shape
    per_group = templates // groups
    length = steps * per_group * used
    grouped = channels.reshape(steps, groups, per_group, used).transpose(1, 0, 2, 3).reshape(groups, length)
    slot = jnp.arange(length, dtype=jnp.int32)
    step = slot // (per_group * used)
    inner = slot % (per_group * used)
    match = (grouped[:, :, None] == station_order[None, None, :]).astype(jnp.int32)
    local = jnp.sum(match, axis=2)
    col = jnp.sum(match * jnp.arange(station_order.shape[0], dtype=jnp.int32), axis=2)
    row = step * (templates * used) + jnp.arange(groups, dtype=jnp.int32)[:, None] * (per_group * used) + inner
    template = slot // used
    code = (row << 14) | (col << 6) | template
    return jnp.where(local > 0, code, -1)


def body(waveform, station_order, library, owner, channels):
    chan_local, time_local = waveform.shape
    num_blocks = time_local // 128
    steps, templates, used = channels.shape
    tap_count = library.shape[2]
    tm_size = lax.axis_size("tm")
    regions = lax.axis_size("region")
    per_group = templates // regions
    held = steps * per_group
    total_time = time_local * tm_size

    rim = lax.ppermute(waveform[:, :256], "tm", [(i, i - 1) for i in range(1, tm_size)])
    rim = jnp.where(jnp.arange(256)[None, :] < tap_count - 1, rim, jnp.zeros_like(rim))

    blocked = waveform.reshape(chan_local, num_blocks, 128)
    rim_blocks = rim.reshape(chan_local, 2, 128)
    extended = jnp.concatenate([blocked, rim_blocks], axis=1)
    windows = jnp.concatenate([extended[:, i : i + num_blocks] for i in range(3)], axis=2)

    vmem = pl.BlockSpec(memory_space=pltpu.VMEM)
    smem = pl.BlockSpec(memory_space=pltpu.SMEM)
    tap_rows = steps * templates * used
    tiles = -(-tap_rows // (16 * tm_size)) * tm_size
    tile = (tiles, 16, 256)
    inv_scale, taps = pl.pallas_call(
        functools.partial(prepare_kernel, steps, tm_size),
        out_shape=[
            jax.ShapeDtypeStruct((chan_local, num_blocks, 128), jnp.float32),
            jax.ShapeDtypeStruct(tile, jnp.float32),
        ],
        in_specs=[smem, vmem, vmem],
        out_specs=[vmem, vmem],
        scratch_shapes=[
            pltpu.VMEM(tile, jnp.bfloat16),
            pltpu.VMEM(tile, jnp.bfloat16),
            pltpu.VMEM((tm_size - 1, tiles // tm_size, 16, 256), jnp.bfloat16),
            pltpu.SemaphoreType.DMA((2, tm_size - 1)),
            pltpu.SemaphoreType.DMA((2, tm_size - 1)),
        ],
        compiler_params=pltpu.CompilerParams(
            collective_id=0, has_side_effects=True, vmem_limit_bytes=40 * 2**20
        ),
        name="prepare",
    )(owner, library.reshape(templates * used, tap_count), windows)
    taps = taps.reshape(tiles * 16, 256)

    codes = pair_lists(station_order, channels, regions)
    me = lax.axis_index("region")

    def partial_sums(group):
        return pl.pallas_call(
            pair_kernel,
            out_shape=jax.ShapeDtypeStruct((held, num_blocks, 128), jnp.float32),
            in_specs=[smem, vmem, vmem, vmem],
            out_specs=vmem,
            scratch_shapes=[
                pltpu.VMEM((held + 1, num_blocks, 128), jnp.float32),
                pltpu.SMEM((held * used + unroll,), jnp.int32),
            ],
            compiler_params=pltpu.CompilerParams(vmem_limit_bytes=40 * 2**20),
            cost_estimate=pl.CostEstimate(flops=held * used * 64 * 384 * 256, bytes_accessed=9 * 2**20, transcendentals=0),
            name="pairs",
        )(lax.dynamic_index_in_dim(codes, group, 0, False), windows, inv_scale, taps)

    arrived = []
    for shift in range(1, regions):
        part = partial_sums((me + shift) % regions)
        arrived.append(lax.ppermute(part, "region", [(i, (i + shift) % regions) for i in range(regions)]))
    arrived.append(partial_sums(me))
    result = pl.pallas_call(
        functools.partial(finish_kernel, total_time, tm_size),
        out_shape=jax.ShapeDtypeStruct((held, num_blocks, 128), jnp.float32),
        in_specs=[vmem] * len(arrived),
        out_specs=vmem,
        scratch_shapes=[
            pltpu.VMEM((held, 128), jnp.float32),
            pltpu.VMEM((tm_size - 1, held, 128), jnp.float32),
            pltpu.SemaphoreType.DMA((tm_size - 1,)),
            pltpu.SemaphoreType.DMA((tm_size - 1,)),
        ],
        compiler_params=pltpu.CompilerParams(
            collective_id=1, has_side_effects=True, vmem_limit_bytes=40 * 2**20
        ),
        name="finish",
    )(*arrived)
    return result.reshape(steps, per_group, time_local)


def solution(mesh):
    in_specs = (P("region", "tm"), P("region"), P("tm", None, None), P(), P())
    out_specs = P(None, "region", "tm")
    return jax.shard_map(body, mesh=mesh, in_specs=in_specs, out_specs=out_specs, check_vma=False)
```

time: 105 us -> 73.7 us (0.70)
  starting transfers between devices: 19.9 us -> 2.83 us
  Pallas kernels: 52.7 us -> 63 us
  local copies, waits for them, and re-layouts: 16.3 us -> 6.34 us
  other arithmetic: 7.98 us -> 1.01 us
  waiting for transfers between devices: 6.93 us -> 0.01 us
    pallas_call x1, Pallas kernels: 6.28 us -> 23.1 us  [body(): pl.pallas_call(functools.partial(prepare_kernel, steps, tm_size), out_sha...]
    ppermute x8 -> x0, starting transfers between devices: 16.3 us -> none  [swap(): return lax.ppermute(block, axis, [(i, i ^ bit) for i in range(count)])]
    pallas_call x2, Pallas kernels: 38.1 us -> 28.8 us  [partial_sums(): pl.pallas_call(pair_kernel, out_shape=jax.ShapeDtypeStruct((held, num_blo...]
    ppermute x8 -> x0, waiting for transfers between devices: 6.92 us -> none  [swap(): return lax.ppermute(block, axis, [(i, i ^ bit) for i in range(count)])]
    rev x1 -> x0, local copies, waits for them, and re-layouts: 4.31 us -> none  [body(): taps = jnp.flip(taps, axis=1).astype(jnp.float32)]
    slice x1, local copies, waits for them, and re-layouts: 3.81 us -> 0.97 us  [body(): extended[:, i:i + num_blocks]]
    reduce_sum x5 -> x1, other arithmetic: 2.9 us -> 0.13 us  [pair_lists(): jnp.sum(match * jnp.arange(station_order.shape[0], dtype=jnp.int32), axis=2)]
    pallas_call x1, Pallas kernels: 8.4 us -> 11.2 us  [body(): pl.pallas_call(functools.partial(finish_kernel, total_time, tm_size), out...]
  transfers between devices with their start and end apart: 10 -> 2, of which waited for: 5 -> 0; matrix products, arithmetic and copies ran while one was open for 13% -> 4% of each run, Pallas kernels for 25% -> 20%
where the time goes in v1:
time: 73.7 us; the launch traced here: 73.4 us
  Pallas kernels  63 us (85%)
  local copies, waits for them, and re-layouts  6.34 us (9%)
  starting transfers between devices  2.83 us (4%)
  other arithmetic  1.01 us (1%)
    pallas_call x2, Pallas kernels, partial_sums(): pl.pallas_call(pair_kernel, out_shape=jax.ShapeDtypeStruct((held, num_blo...  28.8 us
    pallas_call x1, Pallas kernels, body(): pl.pallas_call(functools.partial(prepare_kernel, steps, tm_size), out_sha...  23.1 us
    pallas_call x1, Pallas kernels, body(): pl.pallas_call(functools.partial(finish_kernel, total_time, tm_size), out...  11.2 us
    unnamed x8, local copies, waits for them, and re-layouts  2.63 us
    ppermute x1, starting transfers between devices, body(): lax.ppermute(part, 'region', [(i, (i + shift) % regions) for i in range(r...  1.55 us
  transfers between devices with their start and end apart: 2, of which 0 were waited for; matrix products, arithmetic and copies ran while one was open for 4% of the time, Pallas kernels for 20%

profile of v1, /device:TPU:0, one launch (start us, length us, event | category | flops | bytes accessed | tf_op | source)
XLA Modules:
  0.0 73.4 jit_solution(3393706915711442514)
XLA Ops:
  0.0 0.8 %slice.9 = bf16[96,256]{1,0:T(8,128)(2,1)S(1)} slice(bf16[96,8192]{1,0:T(8,128)(2,1)} %param.5), slice={[0:96], [0:256]} | slice | bytes 98304 | tf_op jit(solution)/shard_map/slice | solution.py:202
  0.8 1.3 %collective-permute-start = (bf16[96,256]{1,0:T(8,128)(2,1)S(1)}, bf16[96,256]{1,0:T(8,128)(2,1)S(1)}, u32[]{:S(2)}, u32[]{:S(2)}) collective-permute-start(bf16[96,256]{1,0:T(8,128)(2,1)S(1)} %slice.9), channel_id=1, source_target_pairs={{2,0},{4,2},{6,4},{8,6},{10,8},{12,10},{14,12},{16,14},{18,16},{20... | collective-permute-start | bytes 147464 | tf_op jit(solution)/shard_map/ppermute | solution.py:202
  2.1 0.7 copy.10
  2.9 0.1 eq.19
  3.0 1.8 %copy.8 = bf16[12,8,64,128]{3,2,1,0:T(8,128)(2,1)S(1)} copy(bf16[12,8,64,128]{3,1,2,0:T(8,128)(2,1)} %bitcast.13) | data formatting | bytes 3145728
  4.8 0.0 copy-start.2
  4.8 0.1 constant_dynamic-update-slice_fusion.1
  4.9 0.5 copy-done.2
  5.5 0.1 fusion.1
  5.6 0.1 compare_select_fusion.1
  5.7 0.0 collective-permute-done
  5.8 0.1 constant_dynamic-update-slice_fusion
  5.8 1.0 %fusion.11 = (bf16[96,64,128]{2,1,0:T(8,128)(2,1)S(1)}, bf16[96,64,128]{2,1,0:T(8,128)(2,1)S(1)}) fusion(bf16[96,66,128]{2,1,0:T(8,128)(2,1)S(1)} %constant_dynamic-update-slice_fusion), kind=kLoop, calls=%fused_computation.30 | loop fusion | bytes 6291456 | tf_op jit(solution)/shard_map/slice | solution.py:208
  6.8 0.0 copy-start
  6.8 0.0 copy-start.1
  6.8 0.8 %pad_maximum_fusion.x_ref = bf16[96,64,384]{2,1,0:T(8,128)(2,1)S(1)} fusion(bf16[96,64,128]{2,1,0:T(8,128)(2,1)S(1)} %get-tuple-element.14, bf16[96,64,128]{2,1,0:T(8,128)(2,1)S(1)} %get-tuple-element.13, bf16[96,64,128]{2,1,0:T(8,128)(2,1)S(1)} %bitcast.12), kind=kLoop, calls=%fused_computation | loop fusion | flops 14155776 | bytes 9437184 | tf_op jit(solution)/shard_map/concatenate | solution.py:208
  7.6 0.1 copy-done
  7.7 0.0 copy-done.1
  7.7 23.1 %prepare.1 = (f32[96,64,128]{2,1,0:T(8,128)S(1)}, f32[48,16,256]{2,1,0:T(8,128)S(1)}) custom-call(s32[4]{0:T(128)S(1)} %copy-done.1, f32[192,200]{1,0:T(8,128)S(1)} %bitcast.10, bf16[96,64,384]{2,1,0:T(8,128)(2,1)S(1)} %pad_maximum_fusion.x_ref), custom_call_target="tpu_custom_call" | custom-call | tf_op jit(solution)/shard_map/prepare/pallas_call | solution.py:215
  30.9 14.1 %pairs.2 = f32[16,64,128]{2,1,0:T(8,128)S(1)} custom-call(s32[384]{0:T(512)S(1)} %get-tuple-element.12.code_ref, bf16[96,64,384]{2,1,0:T(8,128)(2,1)S(1)} %pad_maximum_fusion.x_ref, f32[96,64,128]{2,1,0:T(8,128)S(1)} %get-tuple-element.7.inv_ref, f32[768,256]{1,0:T(8,128)S(1)} %bitcast.8), custom_call_target="tpu_custom_call" | custom-call | flops 2415919104 | bytes 9437184 | tf_op jit(solution)/shard_map/pairs/pallas_call | solution.py:241
  45.0 1.6 %collective-permute-start.1 = (f32[16,64,128]{2,1,0:T(8,128)S(1)}, f32[16,64,128]{2,1,0:T(8,128)S(1)}, u32[]{:S(2)}, u32[]{:S(2)}) collective-permute-start(f32[16,64,128]{2,1,0:T(8,128)S(1)} %pairs.2), channel_id=1, source_target_pairs={{0,1},{1,0},{2,3},{3,2},{4,5},{5,4},{6,7},{7,6},{8,9},{9,8},{10,11... | collective-permute-start | bytes 1572872 | tf_op jit(solution)/shard_map/ppermute | solution.py:258
  46.6 14.6 %pairs.3.refs_1_ = f32[16,64,128]{2,1,0:T(8,128)S(1)} custom-call(s32[384]{0:T(512)S(1)} %get-tuple-element.11.code_ref, bf16[96,64,384]{2,1,0:T(8,128)(2,1)S(1)} %pad_maximum_fusion.x_ref, f32[96,64,128]{2,1,0:T(8,128)S(1)} %get-tuple-element.7.inv_ref, f32[768,256]{1,0:T(8,128)S(1)} %bitcast.9), custom_call_target="tpu_custom_call" | custom-call | flops 2415919104 | bytes 9437184 | tf_op jit(solution)/shard_map/pairs/pallas_call | solution.py:241
  61.2 0.0 collective-permute-done.1.refs_0_
  61.2 11.2 %finish.1 = f32[16,64,128]{2,1,0:T(8,128)S(1)} custom-call(f32[16,64,128]{2,1,0:T(8,128)S(1)} %collective-permute-done.1.refs_0_, f32[16,64,128]{2,1,0:T(8,128)S(1)} %pairs.3.refs_1_), custom_call_target="tpu_custom_call" | custom-call | tf_op jit(solution)/shard_map/finish/pallas_call | solution.py:260
  72.4 1.0 %reshape.66 = f32[4,4,8192]{2,1,0:T(4,128)} reshape(f32[16,64,128]{2,1,0:T(8,128)S(1)} %finish.1) | data formatting | bytes 1048576 | tf_op jit(solution)/shard_map/reshape | solution.py:276
  (7 shorter events, 0.1 us)
Async XLA Ops:
  0.8 4.9 %collective-permute-start = (bf16[96,256]{1,0:T(8,128)(2,1)S(1)}, bf16[96,256]{1,0:T(8,128)(2,1)S(1)}, u32[]{:S(2)}, u32[]{:S(2)}) collective-permute-start(bf16[96,256]{1,0:T(8,128)(2,1)S(1)} %slice.9), channel_id=1, source_target_pairs={{2,0},{4,2},{6,4},{8,6},{10,8},{12,10},{14,12},{16,14},{18,16},{20... | collective-permute-start | bytes 147464 | tf_op jit(solution)/shard_map/ppermute | solution.py:202
  4.8 0.7 copy-start.2
  6.8 0.9 %copy-start = (f32[8,24,200]{2,1,0:T(8,128)S(1)}, f32[8,24,200]{2,1,0:T(8,128)}, u32[]{:S(2)}) copy-start(f32[8,24,200]{2,1,0:T(8,128)} %param.7) | copy-start | bytes 460804
  6.8 0.9 %copy-start.1 = (s32[4]{0:T(128)S(1)}, s32[4]{0:T(128)}, u32[]{:S(2)}) copy-start(s32[4]{0:T(128)} %owner_ref.1) | copy-start | bytes 52
  45.0 16.2 %collective-permute-start.1 = (f32[16,64,128]{2,1,0:T(8,128)S(1)}, f32[16,64,128]{2,1,0:T(8,128)S(1)}, u32[]{:S(2)}, u32[]{:S(2)}) collective-permute-start(f32[16,64,128]{2,1,0:T(8,128)S(1)} %pairs.2), channel_id=1, source_target_pairs={{0,1},{1,0},{2,3},{3,2},{4,5},{5,4},{6,7},{7,6},{8,9},{9,8},{10,11... | collective-permute-start | bytes 1572872 | tf_op jit(solution)/shard_map/ppermute | solution.py:258

commit v2 on v1

--- a/solution.py
+++ b/solution.py
@@ -8,7 +8,7 @@
 
 water_level = 4.0
 eps = 1e-06
-unroll = 8
+unroll = 16
 
 
 def prepare_kernel(steps, count, owner_ref, library_ref, x_ref, inv_ref, out_ref, part, full, got, send_sems, recv_sems):

time: 73.7 us -> 69.2 us (0.939)
  Pallas kernels: 63 us -> 58.1 us
  waiting for transfers between devices: 0.01 us -> 0.9 us
  starting transfers between devices: 2.83 us -> 2.01 us
    pallas_call x2, Pallas kernels: 28.8 us -> 24.6 us  [partial_sums(): pl.pallas_call(pair_kernel, out_shape=jax.ShapeDtypeStruct((held, num_blo...]
    ppermute x1, waiting for transfers between devices: 0.01 us -> 0.9 us  [body(): lax.ppermute(part, 'region', [(i, (i + shift) % regions) for i in range(r...]
    ppermute x1, starting transfers between devices: 1.55 us -> 0.73 us  [body(): lax.ppermute(part, 'region', [(i, (i + shift) % regions) for i in range(r...]
    pallas_call x1, Pallas kernels: 11.2 us -> 10.3 us  [body(): pl.pallas_call(functools.partial(finish_kernel, total_time, tm_size), out...]
  transfers between devices with their start and end apart: 2 -> 2, of which waited for: 0 -> 1; matrix products, arithmetic and copies ran while one was open for 4% -> 4% of each run, Pallas kernels for 20% -> 19%
where the time goes in v2:
time: 69.2 us; the launch traced here: 68.5 us
  Pallas kernels  58.1 us (84%)
  local copies, waits for them, and re-layouts  6.34 us (9%)
  starting transfers between devices  2.01 us (3%)
  other arithmetic  1.01 us (1%)
  waiting for transfers between devices  0.9 us (1%)
    pallas_call x2, Pallas kernels, partial_sums(): pl.pallas_call(pair_kernel, out_shape=jax.ShapeDtypeStruct((held, num_blo...  24.6 us
    pallas_call x1, Pallas kernels, body(): pl.pallas_call(functools.partial(prepare_kernel, steps, tm_size), out_sha...  23.1 us
    pallas_call x1, Pallas kernels, body(): pl.pallas_call(functools.partial(finish_kernel, total_time, tm_size), out...  10.3 us
    unnamed x8, local copies, waits for them, and re-layouts  2.63 us
  transfers between devices with their start and end apart: 2, of which 1 were waited for; matrix products, arithmetic and copies ran while one was open for 4% of the time, Pallas kernels for 19%

profile of v2, /device:TPU:0, one launch (start us, length us, event | category | flops | bytes accessed | tf_op | source)
XLA Modules:
  0.0 68.5 jit_solution(15344108003445229747)
XLA Ops:
  0.0 0.8 %slice.9 = bf16[96,256]{1,0:T(8,128)(2,1)S(1)} slice(bf16[96,8192]{1,0:T(8,128)(2,1)} %param.5), slice={[0:96], [0:256]} | slice | bytes 98304 | tf_op jit(solution)/shard_map/slice | solution.py:202
  0.8 1.3 %collective-permute-start = (bf16[96,256]{1,0:T(8,128)(2,1)S(1)}, bf16[96,256]{1,0:T(8,128)(2,1)S(1)}, u32[]{:S(2)}, u32[]{:S(2)}) collective-permute-start(bf16[96,256]{1,0:T(8,128)(2,1)S(1)} %slice.9), channel_id=1, source_target_pairs={{2,0},{4,2},{6,4},{8,6},{10,8},{12,10},{14,12},{16,14},{18,16},{20... | collective-permute-start | bytes 147464 | tf_op jit(solution)/shard_map/ppermute | solution.py:202
  2.1 0.7 %copy.10 = s32[4,2,4,24]{3,2,0,1:T(4,128)S(1)} copy(s32[4,2,4,24]{3,2,1,0:T(4,128)} %bitcast.15) | data formatting | bytes 6144 | tf_op jit(solution)/shard_map/reshape | solution.py:178
  2.9 0.1 eq.19
  3.0 1.8 %copy.8 = bf16[12,8,64,128]{3,2,1,0:T(8,128)(2,1)S(1)} copy(bf16[12,8,64,128]{3,1,2,0:T(8,128)(2,1)} %bitcast.13) | data formatting | bytes 3145728
  4.8 0.0 copy-start.2
  4.8 0.1 constant_dynamic-update-slice_fusion.1
  4.9 0.5 copy-done.2
  5.5 0.1 fusion.1
  5.6 0.1 compare_select_fusion.1
  5.7 0.0 collective-permute-done
  5.8 0.1 constant_dynamic-update-slice_fusion
  5.8 1.0 %fusion.11 = (bf16[96,64,128]{2,1,0:T(8,128)(2,1)S(1)}, bf16[96,64,128]{2,1,0:T(8,128)(2,1)S(1)}) fusion(bf16[96,66,128]{2,1,0:T(8,128)(2,1)S(1)} %constant_dynamic-update-slice_fusion), kind=kLoop, calls=%fused_computation.30 | loop fusion | bytes 6291456 | tf_op jit(solution)/shard_map/slice | solution.py:208
  6.8 0.0 copy-start
  6.8 0.0 copy-start.1
  6.8 0.8 %pad_maximum_fusion.x_ref = bf16[96,64,384]{2,1,0:T(8,128)(2,1)S(1)} fusion(bf16[96,64,128]{2,1,0:T(8,128)(2,1)S(1)} %get-tuple-element.14, bf16[96,64,128]{2,1,0:T(8,128)(2,1)S(1)} %get-tuple-element.13, bf16[96,64,128]{2,1,0:T(8,128)(2,1)S(1)} %bitcast.12), kind=kLoop, calls=%fused_computation | loop fusion | flops 14155776 | bytes 9437184 | tf_op jit(solution)/shard_map/concatenate | solution.py:208
  7.6 0.1 copy-done
  7.7 0.0 copy-done.1
  7.7 23.1 %prepare.1 = (f32[96,64,128]{2,1,0:T(8,128)S(1)}, f32[48,16,256]{2,1,0:T(8,128)S(1)}) custom-call(s32[4]{0:T(128)S(1)} %copy-done.1, f32[192,200]{1,0:T(8,128)S(1)} %bitcast.10, bf16[96,64,384]{2,1,0:T(8,128)(2,1)S(1)} %pad_maximum_fusion.x_ref), custom_call_target="tpu_custom_call" | custom-call | tf_op jit(solution)/shard_map/prepare/pallas_call | solution.py:215
  30.9 11.5 %pairs.2 = f32[16,64,128]{2,1,0:T(8,128)S(1)} custom-call(s32[384]{0:T(512)S(1)} %get-tuple-element.12.code_ref, bf16[96,64,384]{2,1,0:T(8,128)(2,1)S(1)} %pad_maximum_fusion.x_ref, f32[96,64,128]{2,1,0:T(8,128)S(1)} %get-tuple-element.7.inv_ref, f32[768,256]{1,0:T(8,128)S(1)} %bitcast.8), custom_call_target="tpu_custom_call" | custom-call | flops 2415919104 | bytes 9437184 | tf_op jit(solution)/shard_map/pairs/pallas_call | solution.py:241
  42.4 0.7 %collective-permute-start.1 = (f32[16,64,128]{2,1,0:T(8,128)S(1)}, f32[16,64,128]{2,1,0:T(8,128)S(1)}, u32[]{:S(2)}, u32[]{:S(2)}) collective-permute-start(f32[16,64,128]{2,1,0:T(8,128)S(1)} %pairs.2), channel_id=1, source_target_pairs={{0,1},{1,0},{2,3},{3,2},{4,5},{5,4},{6,7},{7,6},{8,9},{9,8},{10,11... | collective-permute-start | bytes 1572872 | tf_op jit(solution)/shard_map/ppermute | solution.py:258
  43.1 13.1 %pairs.3.refs_1_ = f32[16,64,128]{2,1,0:T(8,128)S(1)} custom-call(s32[384]{0:T(512)S(1)} %get-tuple-element.11.code_ref, bf16[96,64,384]{2,1,0:T(8,128)(2,1)S(1)} %pad_maximum_fusion.x_ref, f32[96,64,128]{2,1,0:T(8,128)S(1)} %get-tuple-element.7.inv_ref, f32[768,256]{1,0:T(8,128)S(1)} %bitcast.9), custom_call_target="tpu_custom_call" | custom-call | flops 2415919104 | bytes 9437184 | tf_op jit(solution)/shard_map/pairs/pallas_call | solution.py:241
  56.3 0.9 %collective-permute-done.1.refs_0_ = f32[16,64,128]{2,1,0:T(8,128)S(1)} collective-permute-done((f32[16,64,128]{2,1,0:T(8,128)S(1)}, f32[16,64,128]{2,1,0:T(8,128)S(1)}, u32[]{:S(2)}, u32[]{:S(2)}) %collective-permute-start.1) | collective-permute-done | bytes 524320 | tf_op jit(solution)/shard_map/ppermute | solution.py:258
  57.2 10.3 %finish.1 = f32[16,64,128]{2,1,0:T(8,128)S(1)} custom-call(f32[16,64,128]{2,1,0:T(8,128)S(1)} %collective-permute-done.1.refs_0_, f32[16,64,128]{2,1,0:T(8,128)S(1)} %pairs.3.refs_1_), custom_call_target="tpu_custom_call" | custom-call | tf_op jit(solution)/shard_map/finish/pallas_call | solution.py:260
  67.5 1.0 %reshape.66 = f32[4,4,8192]{2,1,0:T(4,128)} reshape(f32[16,64,128]{2,1,0:T(8,128)S(1)} %finish.1) | data formatting | bytes 1048576 | tf_op jit(solution)/shard_map/reshape | solution.py:276
  (7 shorter events, 0.1 us)
Async XLA Ops:
  0.8 4.9 %collective-permute-start = (bf16[96,256]{1,0:T(8,128)(2,1)S(1)}, bf16[96,256]{1,0:T(8,128)(2,1)S(1)}, u32[]{:S(2)}, u32[]{:S(2)}) collective-permute-start(bf16[96,256]{1,0:T(8,128)(2,1)S(1)} %slice.9), channel_id=1, source_target_pairs={{2,0},{4,2},{6,4},{8,6},{10,8},{12,10},{14,12},{16,14},{18,16},{20... | collective-permute-start | bytes 147464 | tf_op jit(solution)/shard_map/ppermute | solution.py:202
  4.8 0.7 copy-start.2
  6.8 0.9 %copy-start = (f32[8,24,200]{2,1,0:T(8,128)S(1)}, f32[8,24,200]{2,1,0:T(8,128)}, u32[]{:S(2)}) copy-start(f32[8,24,200]{2,1,0:T(8,128)} %param.7) | copy-start | bytes 460804
  6.8 0.9 %copy-start.1 = (s32[4]{0:T(128)S(1)}, s32[4]{0:T(128)}, u32[]{:S(2)}) copy-start(s32[4]{0:T(128)} %owner_ref.1) | copy-start | bytes 52
  42.4 14.8 %collective-permute-start.1 = (f32[16,64,128]{2,1,0:T(8,128)S(1)}, f32[16,64,128]{2,1,0:T(8,128)S(1)}, u32[]{:S(2)}, u32[]{:S(2)}) collective-permute-start(f32[16,64,128]{2,1,0:T(8,128)S(1)} %pairs.2), channel_id=1, source_target_pairs={{0,1},{1,0},{2,3},{3,2},{4,5},{5,4},{6,7},{7,6},{8,9},{9,8},{10,11... | collective-permute-start | bytes 1572872 | tf_op jit(solution)/shard_map/ppermute | solution.py:258
